TPU v7x, 256 devices: a whole 4x4x8 slice. The times are simulated.
256 devices in a mesh: section: 32 (over z_hi, x, core), rep: 8 (over z_lo, y).
Axes of the slice: x: 4, y: 4, z: 8 (z_hi: 4, z_lo: 2; z = z_hi * 2 + z_lo), core: 2. Of those that a mesh axis runs over, the one named last changes fastest.
Arguments:
- features: bfloat16 [65536, 256], P(('section', 'rep')), may hold values from -6 to 6
- tiles: bfloat16 [32, 8, 64, 256, 256], P('section', 'rep'), may hold values from -0.0625 to 0.0625
- tile_rows: int32 [32, 8, 64], P('section', 'rep'), may hold values from 0 to 7, as said below
- tile_cols: int32 [32, 8, 64], P('section', 'rep'), may hold values from 0 to 31, as said below
- tile_count: int32 [32, 8], P('section', 'rep'), may hold values from 16 to 64, as said below
- weight: bfloat16 [256, 256], replicated, may hold values from -0.375 to 0.375
- cotangent: bfloat16 [65536, 256], P(('section', 'rep')), may hold values from -6 to 6
Outputs:
- activated: bfloat16 [65536, 256], P(('section', 'rep'))
- weight_grad: float32 [256, 256], replicated
- feature_grad: bfloat16 [65536, 256], P(('section', 'rep'))
Inputs may be any that keep to these rules, and one draw needn't show every extreme that they name: `tile_rows`: on each device the first tile_count slots name distinct pairs of tile row and tile column; slots from tile_count on are unused, whatever they hold. `tile_cols`: tile column within the column set of the device's rep index, which has 32 * 8 / 8 tiles. `tile_count`: some device uses all 64 slots.
All inputs are finite; a program needn't handle non-finite values.
Results may differ from a plain program's by a relative error of at most 0.0065.
Values may be sent and summed in bfloat16 or wider, within the bound.
A program may use at most 128 MiB of HBM per device.

v0:
```python
import jax
import jax.numpy as jnp
from jax import lax
from jax.sharding import PartitionSpec as P


def silu_slope(pre_act):
    sigma = jax.nn.sigmoid(pre_act)
    return sigma * (1.0 + pre_act * (1.0 - sigma))


def per_device(features, tiles, tile_rows, tile_cols, tile_count, weight, cotangent):
    highest = lax.Precision.HIGHEST
    section_tiles = tiles[0, 0]
    row_ids = tile_rows[0, 0]
    col_ids = tile_cols[0, 0]
    live_count = tile_count[0, 0]
    tile_size = section_tiles.shape[-1]
    own_rows = features.shape[0]
    feature_width = features.shape[1]
    slot_total = row_ids.shape[0]
    block_rows = own_rows * lax.axis_size("rep")
    row_tiles = block_rows // tile_size
    gathered = lax.all_gather(features, "section", axis=0, tiled=True)
    col_tiles = gathered.shape[0] // tile_size
    in_use = lax.iota(jnp.int32, slot_total) < live_count
    selected = gathered.reshape(col_tiles, tile_size, feature_width)[col_ids]
    products = jnp.einsum(
        "kij,kjf->kif", section_tiles, selected, preferred_element_type=jnp.float32
    )
    row_hot = (
        (row_ids[:, None] == lax.iota(jnp.int32, row_tiles)[None, :]) & in_use[:, None]
    ).astype(jnp.float32)
    partial_value = jnp.einsum("kt,kif->tif", row_hot, products, precision=highest).reshape(
        block_rows, feature_width
    )
    aggregate = lax.psum(partial_value, "rep").astype(jnp.bfloat16)
    block_cot = lax.all_gather(cotangent, "rep", axis=0, tiled=True)
    pre_act = jnp.dot(aggregate, weight, preferred_element_type=jnp.float32)
    block_act = jax.nn.silu(pre_act).astype(jnp.bfloat16)
    activated = lax.dynamic_slice_in_dim(block_act, lax.axis_index("rep") * own_rows, own_rows, 0)
    pre_grad = (block_cot.astype(jnp.float32) * silu_slope(pre_act)).astype(jnp.bfloat16)
    weight_terms = lax.dot_general(
        aggregate, pre_grad, (((0,), (0,)), ((), ())), preferred_element_type=jnp.float32
    )
    weight_grad = lax.psum(weight_terms, "section")
    back_rows = jnp.dot(pre_grad, weight.T, preferred_element_type=jnp.float32).astype(jnp.bfloat16)
    chosen = back_rows.reshape(row_tiles, tile_size, feature_width)[row_ids]
    backward = jnp.einsum("kji,kjf->kif", section_tiles, chosen, preferred_element_type=jnp.float32)
    col_hot = (
        (col_ids[:, None] == lax.iota(jnp.int32, col_tiles)[None, :]) & in_use[:, None]
    ).astype(jnp.float32)
    column_terms = jnp.einsum("kc,kif->cif", col_hot, backward, precision=highest).reshape(
        col_tiles * tile_size, feature_width
    )
    feature_grad = lax.psum_scatter(column_terms, "section", scatter_dimension=0, tiled=True)
    return (activated, weight_grad, feature_grad.astype(jnp.bfloat16))


def solution(mesh):
    placed = (
        P(("section", "rep"), None),
        P("section", "rep", None, None, None),
        P("section", "rep", None),
        P("section", "rep", None),
        P("section", "rep"),
        P(),
        P(("section", "rep"), None),
    )
    return jax.shard_map(
        per_device,
        mesh=mesh,
        in_specs=placed,
        out_specs=(P(("section", "rep"), None), P(), P(("section", "rep"), None)),
        check_vma=False,
    )
```

profile of v0, /device:TPU:1, one launch (start us, length us, event | category | flops | bytes accessed | tf_op | source)
XLA Modules:
  0.0 666.2 jit_solution(5167392282134920325)
XLA Ops:
  7.2 0.0 copy-start
  7.2 0.0 all-gather.3.cloned.1.call-start
  7.2 0.7 all-gather.3.cloned.1.call-update
  7.9 0.0 all-gather.5.cloned.1.call-start
  8.0 0.7 all-gather.5.cloned.1.call-update
  8.7 0.0 reduce-scatter.2.cloned.1.call-start
  9.4 0.7 fusion.23
  10.0 0.7 fusion.24
  10.7 64.6 %all-gather.3.cloned.1.call-done = bf16[8192,256]{1,0:T(8,128)(2,1)} async-done(((bf16[256,256]{1,0:T(8,128)(2,1)}), bf16[8192,256]{1,0:T(8,128)(2,1)}) %all-gather.3.cloned.1.call-update) | async-done | bytes 4194320 | tf_op jit(solution)/shard_map/all_gather | solution.py:24
  75.3 7.7 %gather_fusion = bf16[64,256,256]{2,1,0:T(8,128)(2,1)} fusion(bf16[32,256,256]{2,1,0:T(8,128)(2,1)} %bitcast.43, s32[1024]{0:T(1024)S(1)} %pad_clamp_fusion.1), kind=kCustom, calls=%fused_computation | custom fusion | bytes 16777472 | tf_op jit(solution)/shard_map/gather | solution.py:27
  83.0 13.7 %fusion.6 = f32[64,256,256]{2,1,0:T(8,128)} fusion(bf16[64,256,256]{2,1,0:T(8,128)(2,1)} %gather_fusion, bf16[1,1,64,256,256]{4,3,2,1,0:T(8,128)(2,1)} %param.8), kind=kOutput, calls=%fused_computation.8 | convolution fusion | flops 2147483648 | bytes 33554432 | tf_op jit(solution)/shard_map/kij,kjf->kif/dot_general | solution.py:28
  96.7 17.8 %copy.12 = f32[64,256,256]{1,0,2:T(8,128)} copy(f32[64,256,256]{2,1,0:T(8,128)} %fusion.6) | data formatting | bytes 33554432 | tf_op jit(solution)/shard_map/kij,kjf->kif/dot_general | solution.py:28
  114.5 9.0 %fusion.2 = f32[8,256,256]{2,0,1:T(8,128)S(1)} fusion(f32[64,256,256]{1,0,2:T(8,128)} %copy.12, s32[64]{0:T(128)S(1)} %bitcast.45, pred[64]{0:T(512)(128)(4,1)S(1)} %iota_compare_fusion.2), kind=kOutput, calls=%fused_computation.4 | convolution fusion | flops 402654208 | bytes 18874688 | tf_op jit(solution)/shard_map/kt,kif->tif/dot_general | solution.py:34
  123.5 0.7 copy.10
  124.2 62.8 %all-reduce.4 = bf16[2048,256]{1,0:T(8,128)(2,1)S(1)} all-reduce(f32[2048,256]{1,0:T(8,128)S(1)} %bitcast.44), channel_id=1, replica_groups=mesh['section'=32,'rep'=8] {'rep'}, use_global_device_ids=true, to_apply=%region_0.0 | all-reduce | flops 524288 | bytes 3145728 | tf_op jit(solution)/shard_map/psum | solution.py:37
  187.0 0.0 all-gather.5.cloned.1.call-done
  187.1 4.1 multiply_convert_fusion
  191.2 0.5 convolution_convert_fusion
  191.7 5.5 gather_fusion.1
  197.2 13.9 %fusion.4 = f32[64,256,256]{2,1,0:T(8,128)} fusion(bf16[64,256,256]{2,1,0:T(8,128)(2,1)} %gather_fusion.1, bf16[1,1,64,256,256]{4,3,2,1,0:T(8,128)(2,1)} %param.8), kind=kOutput, calls=%fused_computation.6 | convolution fusion | flops 2147483648 | bytes 33554432 | tf_op jit(solution)/shard_map/kji,kjf->kif/dot_general | solution.py:49
  211.1 17.8 %copy.13 = f32[64,256,256]{1,0,2:T(8,128)} copy(f32[64,256,256]{2,1,0:T(8,128)} %fusion.4) | data formatting | bytes 33554432 | tf_op jit(solution)/shard_map/kji,kjf->kif/dot_general | solution.py:49
  228.8 10.4 %fusion = f32[32,256,256]{2,0,1:T(8,128)S(1)} fusion(f32[64,256,256]{1,0,2:T(8,128)} %copy.13, s32[64]{0:T(128)S(1)} %bitcast.46, pred[64]{0:T(512)(128)(4,1)S(1)} %iota_compare_fusion.2), kind=kOutput, calls=%fused_computation.2 | convolution fusion | flops 1610616832 | bytes 25166144 | tf_op jit(solution)/shard_map/kc,kif->cif/dot_general | solution.py:53
  239.3 8.1 %copy.11 = f32[32,256,256]{2,1,0:T(8,128)} copy(f32[32,256,256]{2,0,1:T(8,128)S(1)} %fusion) | data formatting | bytes 16777216 | tf_op jit(solution)/shard_map/kc,kif->cif/dot_general | solution.py:53
  247.3 0.0 reduce-scatter.2.cloned.1.call-update
  247.4 0.0 all-reduce.3.cloned.1.call-start
  247.4 1.2 fusion.25
  248.6 0.0 all-reduce.3.cloned.1.call-update
  248.6 1.7 fusion.12
  250.3 123.6 %reduce-scatter.2.cloned.1.call-done = f32[256,256]{1,0:T(8,128)} async-done(((f32[8192,256]{1,0:T(8,128)}), f32[256,256]{1,0:T(8,128)}) %reduce-scatter.2.cloned.1.call-update) | async-done | bytes 262160 | tf_op jit(solution)/shard_map/reduce_scatter | solution.py:56
  374.0 1.6 convert_element_type.25
  375.6 282.4 %all-reduce.3.cloned.1.call-done = f32[256,256]{1,0:T(8,128)} async-done(((f32[256,256]{1,0:T(8,128)}), f32[256,256]{1,0:T(8,128)}) %all-reduce.3.cloned.1.call-update) | async-done | bytes 262160 | tf_op jit(solution)/shard_map/psum | solution.py:46
  658.0 1.7 copy.18
  (10 shorter events, 0.0 us)
Async XLA Ops:
  7.2 179.9 %copy-start = (bf16[256,256]{1,0:T(8,128)(2,1)S(1)}, bf16[256,256]{1,0:T(8,128)(2,1)}, u32[]{:S(2)}) copy-start(bf16[256,256]{1,0:T(8,128)(2,1)} %param.12) | copy-start | bytes 393220
  7.2 68.1 %all-gather.3.cloned.1.call-start = ((), (), s32[]{:S(2)}) async-start(), calls=%async_computation.1 | async-start | bytes 4325376 | tf_op jit(solution)/shard_map/all_gather | solution.py:24
  7.9 179.1 %all-gather.5.cloned.1.call-start = ((), (), s32[]{:S(2)}) async-start(), calls=%async_computation.2 | async-start | bytes 1179648 | tf_op jit(solution)/shard_map/all_gather | solution.py:38
  8.7 365.3 %reduce-scatter.2.cloned.1.call-start = ((), (), s32[]{:S(2)}) async-start(), calls=%async_computation.4 | async-start | bytes 8650752 | tf_op jit(solution)/shard_map/reduce_scatter | solution.py:56
  96.7 17.8 %copy-start.2 = (s32[1,1,64]{2,1,0:T(1,128)S(1)}, s32[1,1,64]{2,1,0:T(1,128)}, u32[]{:S(2)}) copy-start(s32[1,1,64]{2,1,0:T(1,128)} %param.9) | copy-start | bytes 772
  211.1 17.8 %copy-start.3 = (s32[1,1,64]{2,1,0:T(1,128)S(1)}, s32[1,1,64]{2,1,0:T(1,128)}, u32[]{:S(2)}) copy-start(s32[1,1,64]{2,1,0:T(1,128)} %param.10) | copy-start | bytes 772
  239.2 420.4 %copy-start.1 = (bf16[256,256]{1,0:T(8,128)(2,1)S(1)}, bf16[256,256]{1,0:T(8,128)(2,1)}, u32[]{:S(2)}) copy-start(bf16[256,256]{1,0:T(8,128)(2,1)} %param.12) | copy-start | bytes 393220
  247.4 410.6 %all-reduce.3.cloned.1.call-start = ((), (), s32[]{:S(2)}) async-start(), calls=%async_computation.3 | async-start | bytes 524288 | tf_op jit(solution)/shard_map/psum | solution.py:46
Sparse Core Ops, SparseCore 0:
  10.6 64.6 all-gather.2
  77.0 33.6 all-gather.4
  247.5 126.4 reduce-scatter.1
  377.2 280.7 all-reduce.2
where the time goes:
time: 667 us; the launch traced here: 666 us
  waiting for transfers between devices  472 us (71%)
  blocking collectives  62.8 us (9%)
  local copies, waits for them, and re-layouts  59.2 us (9%)
  matrix products  52.8 us (8%)
  between operations  14.5 us (2%)
    psum x1, waiting for transfers between devices, per_device(): weight_grad = lax.psum(weight_terms, 'section')  282 us
    reduce_scatter x1, waiting for transfers between devices, per_device(): lax.psum_scatter(column_terms, 'section', scatter_dimension=0, tiled=True)  124 us
    all_gather x1, waiting for transfers between devices, per_device(): gathered = lax.all_gather(features, 'section', axis=0, tiled=True)  64.6 us
    psum x1, blocking collectives, per_device(): aggregate = lax.psum(partial_value, 'rep').astype(jnp.bfloat16)  62.8 us
    dot_general x1, local copies, waits for them, and re-layouts, per_device(): jnp.einsum('kij,kjf->kif', section_tiles, selected, preferred_element_typ...  17.8 us
    dot_general x1, local copies, waits for them, and re-layouts, per_device(): jnp.einsum('kji,kjf->kif', section_tiles, chosen, preferred_element_type=...  17.8 us
    dot_general x1, matrix products, per_device(): jnp.einsum('kji,kjf->kif', section_tiles, chosen, preferred_element_type=...  13.9 us
    dot_general x1, matrix products, per_device(): jnp.einsum('kij,kjf->kif', section_tiles, selected, preferred_element_typ...  13.7 us
  transfers between devices with their start and end apart: 4, of which 3 were waited for; matrix products, arithmetic and copies ran while one was open for 8% of the time, Pallas kernels for 0%

commit v1 on v0

v1 whole, which is shorter than its diff:
```python
import jax
import jax.numpy as jnp
from jax import lax
from jax.experimental import pallas as pl
from jax.experimental.pallas import tpu as pltpu
from jax.sharding import PartitionSpec as P

f32, bf16 = jnp.float32, jnp.bfloat16
T = 256
SLOTS = 64
STEP = (0, 1, -1, 2)
FWD = ((0, 64), (64, 64), (128, 64), (192, 64))
BWD = ((0, 64), (64, 64), (128, 64), (192, 64))
UNROLL = 32


def transpose(v):
    return v.T


def kernel(
    feat_ref, tiles_ref, rows_ref, cols_ref, count_ref, weight_ref, cot_ref,
    act_ref, wgrad_ref, fgrad_ref,
    tiles, tiles_t, prefix, rs_send, rs_recv, agg_own, agg_t, wt, cot_t,
    c_send, c_recv, comb, xh_send, xh_recv, xf_send, xf_recv, z_send, z_recv, fg_t,
    w0, w1r, w1, w2r, w2, w3r, w4, w5, w6, w7, table_v, table,
    send_sem, recv_sem, local_sem, *per_slice,
):
    gathered, row_grads = per_slice[: len(FWD)], per_slice[len(FWD) :]
    section, rep = lax.axis_index("section"), lax.axis_index("rep")
    zh, x, c = section // 8, (section // 2) % 4, section % 2
    zl, y = rep // 4, rep % 4

    def at(dzh=0, dx=0, dc=0, dzl=0, dy=0):
        return (
            (((zh + dzh + 4) % 4) * 4 + (x + dx + 4) % 4) * 2 + (c + dc) % 2,
            ((zl + dzl) % 2) * 4 + (y + dy + 4) % 4,
        )

    rep_offs = [dict(dzl=e // 4, dy=STEP[e % 4]) for e in range(8)]
    partners = (
        [dict(dx=STEP[i]) for i in (1, 2, 3)]
        + [dict(dzh=STEP[i]) for i in (1, 2, 3)]
        + [dict(dc=1)]
        + rep_offs[1:]
    )
    back = (0, 2, 1, 3)
    channels = {}

    def send(key, src, dst, off):
        i = len(channels)
        copy = pltpu.make_async_remote_copy(
            src_ref=src, dst_ref=dst, send_sem=send_sem.at[i], recv_sem=recv_sem.at[i],
            device_id=at(**off), device_id_type=pl.DeviceIdType.MESH,
        )
        copy.start()
        channels[key] = copy

    def recv(key):
        channels[key].wait_recv()

    barrier = pltpu.get_barrier_semaphore()
    for off in partners:
        pl.semaphore_signal(barrier, inc=1, device_id=at(**off), device_id_type=pl.DeviceIdType.MESH)
    loads = [
        pltpu.make_async_copy(tiles_ref.at[pl.ds(i * 8, 8)], tiles.at[pl.ds(i * 8, 8)], local_sem.at[i])
        for i in range(8)
    ]
    for load in loads:
        load.start()
    feat_t = transpose(feat_ref[...])
    for q, (a, n) in enumerate(FWD):
        gathered[q][0] = feat_t[a : a + n]
    pl.semaphore_wait(barrier, len(partners))

    def x_full(q, dz):
        g = gathered[q]
        send(("xf", q, dz, 1), g.at[dz * 4], g.at[dz * 4 + 2], dict(dx=1))
        send(("xf", q, dz, -1), g.at[dz * 4], g.at[dz * 4 + 1], dict(dx=-1))

    for q in range(len(FWD)):
        g = gathered[q]
        for dz in (1, 2, 3):
            send(("z", q, dz), g.at[0], g.at[back[dz] * 4], dict(dzh=STEP[dz]))
        x_full(q, 0)

    def make_tables():
        lane = lax.broadcasted_iota(jnp.int32, (SLOTS, SLOTS), 1)
        sub = lax.broadcasted_iota(jnp.int32, (SLOTS, SLOTS), 0)
        count = count_ref[0, 0]
        r_l = jnp.broadcast_to(rows_ref[...], (SLOTS, SLOTS))
        c_l = jnp.broadcast_to(cols_ref[...], (SLOTS, SLOTS))
        r_s = r_l.astype(f32).T.astype(jnp.int32)
        c_s = c_l.astype(f32).T.astype(jnp.int32)
        live_s = sub < count
        lane_w = lax.broadcasted_iota(jnp.int32, (SLOTS, 128), 1)
        sub_w = lax.broadcasted_iota(jnp.int32, (SLOTS, 128), 0)

        def ring(delta):
            d = (delta + 8) % 4
            return jnp.where(d == 2, 3, jnp.where(d == 3, 2, d))

        def one(major_l, minor_l, major_s, minor_s, width, other, base):
            key_l = jnp.where(lane < count, major_l * width + minor_l, 1000 + lane)
            key_s = jnp.where(live_s, major_s * width + minor_s, 1000 + sub)
            before = key_l < key_s
            rank = jnp.sum(before.astype(f32), axis=1, keepdims=True)
            same = jnp.sum((before & (major_l == major_s)).astype(f32), axis=1, keepdims=True)
            hot = jnp.broadcast_to(rank, (SLOTS, 128)) == lane_w.astype(f32)
            first = jnp.broadcast_to((same == 0).astype(f32), (SLOTS, 128))

            def pick(v):
                return jnp.sum(jnp.where(hot, v, 0.0), axis=0, keepdims=True).astype(jnp.int32)

            major_w = jnp.broadcast_to(major_s[:, :1], (SLOTS, 128))
            live_w = sub_w < count
            upto = jnp.sum((live_w & (major_w <= lane_w)).astype(f32), axis=0, keepdims=True)
            equal = jnp.sum((live_w & (major_w == lane_w)).astype(f32), axis=0, keepdims=True)
            last = jnp.where(equal > 0, upto - 1.0, -1.0).astype(jnp.int32)
            table_v[base : base + 1, :] = pick(sub_w.astype(f32))
            table_v[base + 1 : base + 2, :] = pick(jnp.broadcast_to(other[:, :1].astype(f32), (SLOTS, 128)))
            table_v[base + 2 : base + 3, :] = pick(first)
            table_v[base + 3 : base + 4, :] = last

        where_col = ((c_s + c) % 2) * 16 + ring(c_s // 8 - zh) * 4 + ring((c_s // 2) % 4 - x)
        where_row = ((r_s // 4 + zl) % 2) * 4 + ring(r_s % 4 - y)
        one(r_l, c_l, r_s, c_s, 32, where_col, 0)
        one(c_l, r_l, c_s, r_s, 8, where_row, 4)

    make_tables()
    to_smem = pltpu.make_async_copy(table_v, table, local_sem.at[8])
    to_smem.start()
    for load in loads:
        load.wait()

    def turn(first, number):
        def step(i, carry):
            for u in range(4):
                k = first + i * 4 + u
                tiles_t[k] = transpose(tiles[k])
            return carry

        lax.fori_loop(0, number // 4, step, 0)

    turn(0, 32)
    wt[...] = transpose(weight_ref[...])
    cot_t[...] = transpose(cot_ref[...])

    def products(source, matrices, base, n):
        def step(i, total):
            for u in range(UNROLL):
                p = i * UNROLL + u
                keep = jnp.where(table[base + 2, p] == 1, 0.0, 1.0)
                s = jnp.clip(table[base + 1, p], 0, source.shape[0] - 1)
                k = jnp.clip(table[base, p], 0, SLOTS - 1)
                total = total * keep + jnp.dot(source[s], matrices[k], preferred_element_type=f32)
                prefix[p, :n] = total
            return total

        lax.fori_loop(0, SLOTS // UNROLL, step, jnp.zeros((n, T), f32))

    def group(base, index, n):
        last = table[base + 3, index]
        return prefix[jnp.clip(last, 0, SLOTS - 1), :n] * jnp.where(last >= 0, 1.0, 0.0)

    def stage_x(q):
        g, n = gathered[q], FWD[q][1]
        h = n // 2
        for dz in (1, 2, 3):
            recv(("z", q, dz))
            x_full(q, back[dz])
        for dz in range(4):
            recv(("xf", q, dz, 1))
            send(("xh", q, dz, 1), g.at[dz * 4 + 2, pl.ds(0, h)], g.at[dz * 4 + 3, pl.ds(0, h)], dict(dx=1))
            recv(("xf", q, dz, -1))
            send(("xh", q, dz, -1), g.at[dz * 4 + 1, pl.ds(h, h)], g.at[dz * 4 + 3, pl.ds(h, h)], dict(dx=-1))

    def stage_core(q):
        g = gathered[q]
        for dz in range(4):
            recv(("xh", q, dz, 1))
            recv(("xh", q, dz, -1))
            send(("core", q, dz), g.at[pl.ds(dz * 4, 4)], g.at[pl.ds(16 + dz * 4, 4)], dict(dc=1))

    def stage_products(q):
        a, n = FWD[q]
        for dz in range(4):
            recv(("core", q, dz))
        products(gathered[q], tiles_t, 0, n)
        for e in (7, 3, 6, 5, 2, 1, 4):
            owner = at(**rep_offs[e])[1]
            rs_send[e, a : a + n] = group(0, owner, n).astype(bf16)
            to = (e // 4) * 4 + back[e % 4]
            send(("rs", q, e), rs_send.at[e, pl.ds(a, n)], rs_recv.at[to, pl.ds(a, n)], rep_offs[e])
        agg_own[a : a + n] = group(0, rep, n)

    for q in range(len(FWD) + 1):
        if q < len(FWD):
            stage_x(q)
        if q == 0:
            turn(32, 32)
            to_smem.wait()
        if q >= 1:
            stage_core(q - 1)
            stage_products(q - 1)

    for q, (a, n) in enumerate(FWD):
        for e in range(1, 8):
            recv(("rs", q, e))
        total = agg_own[a : a + n]
        for e in range(1, 8):
            total = total + rs_recv[e, a : a + n].astype(f32)
        agg_t[a : a + n] = total.astype(bf16)

    pre = jnp.dot(wt[...], agg_t[...], preferred_element_type=f32)
    sigma = jax.nn.sigmoid(pre)
    pre_grad = (cot_t[...].astype(f32) * (sigma * (1.0 + pre * (1.0 - sigma)))).astype(bf16)
    for q, (a, n) in enumerate(BWD):
        row_grads[q][0] = jnp.dot(weight_ref[a : a + n], pre_grad, preferred_element_type=f32).astype(bf16)
        for e in (7, 3, 6, 5, 2, 1, 4):
            to = (e // 4) * 4 + back[e % 4]
            send(("ag", q, e), row_grads[q].at[0], row_grads[q].at[to], rep_offs[e])
    act_ref[...] = (pre * sigma).T.astype(bf16)
    w0[...] = lax.dot_general(agg_t[...], pre_grad, (((1,), (1,)), ((), ())), preferred_element_type=f32)

    def aligned(v, k):
        return pl.ds(pl.multiple_of(v * k, k), k)

    def weight_1():
        send("w1", w0.at[aligned(1 - c, 128)], w1r, dict(dc=1))

    def weight_2():
        recv("w1")
        w1[...] = w0[aligned(c, 128), :] + w1r[...]
        for i in (3, 1, 2):
            send(("w2", i), w1.at[aligned((x + STEP[i] + 4) % 4, 32)], w2r.at[back[i] - 1], dict(dx=STEP[i]))

    def weight_3():
        total = w1[aligned(x, 32), :]
        for i in (1, 2, 3):
            recv(("w2", i))
        for i in (1, 2, 3):
            total = total + w2r[i - 1]
        w2[...] = total
        for i in (3, 1, 2):
            send(("w3", i), w2.at[aligned((zh + STEP[i] + 4) % 4, 8)], w3r.at[back[i] - 1], dict(dzh=STEP[i]))

    def weight_4():
        total = w2[aligned(zh, 8), :]
        for i in (1, 2, 3):
            recv(("w3", i))
        for i in (1, 2, 3):
            total = total + w3r[i - 1]
        w4[rep] = total
        for e in range(1, 8):
            send(("w4", e), w4.at[rep], w4.at[rep], rep_offs[e])

    def weight_5():
        for e in range(1, 8):
            recv(("w4", e))
        w5[aligned(zh, 8), :] = jnp.sum(w4[...], axis=0)
        for i in (3, 1, 2):
            send(("w5", i), w5.at[aligned(zh, 8)], w5.at[aligned(zh, 8)], dict(dzh=STEP[i]))

    def weight_6():
        for i in (1, 2, 3):
            recv(("w5", i))
        w6[aligned(x, 32), :] = w5[...]
        for i in (3, 1, 2):
            send(("w6", i), w6.at[aligned(x, 32)], w6.at[aligned(x, 32)], dict(dx=STEP[i]))

    def weight_7():
        for i in (1, 2, 3):
            recv(("w6", i))
        w7[aligned(c, 128), :] = w6[...]
        send("w7", w7.at[aligned(c, 128)], w7.at[aligned(c, 128)], dict(dc=1))

    def weight_8():
        recv("w7")
        wgrad_ref[...] = w7[...]

    def back_products(q):
        a, n = BWD[q]
        for e in range(1, 8):
            recv(("ag", q, e))
        products(row_grads[q], tiles, 4, n)
        for dz in (3, 1, 2, 0):
            for dx in (3, 1, 2, 0):
                other = at(dzh=STEP[dz], dx=STEP[dx], dc=1)[0]
                c_send[dz * 4 + dx, a : a + n] = group(4, other, n).astype(bf16)
            part = (pl.ds(dz * 4, 4), pl.ds(a, n))
            send(("bc", q, dz), c_send.at[part], c_recv.at[part], dict(dc=1))
        for dz in (3, 1, 2, 0):
            for dx in (3, 1, 2, 0):
                own = at(dzh=STEP[dz], dx=STEP[dx])[0]
                comb[dz * 4 + dx, a : a + n] = group(4, own, n)

    def both(i, a, n):
        return comb[i, a : a + n] + c_recv[i, a : a + n].astype(f32)

    def back_xh(q):
        a, n = BWD[q]
        h = n // 2
        for dz in range(4):
            recv(("bc", q, dz))
            xh_send[dz, a : a + n] = both(dz * 4 + 3, a, n).astype(bf16)
        for k, d, s in ((0, 1, a), (1, -1, a + h)):
            send(("bxh", q, k), xh_send.at[:, pl.ds(s, h)], xh_recv.at[:, pl.ds(s, h)], dict(dx=d))

    def back_xf(q):
        a, n = BWD[q]
        h = n // 2
        for k, d, s in ((0, 1, a), (1, -1, a + h)):
            recv(("bxh", q, k))
            o = a + h if k == 0 else a
            for dz in range(4):
                i = dz * 4 + 1 + k
                xf_send[k, dz, s : s + h] = (both(i, s, h) + xh_recv[dz, s : s + h].astype(f32)).astype(bf16)
                xf_send[k, dz, o : o + h] = both(i, o, h).astype(bf16)
            part = (slice(None), pl.ds(a, n))
            send(("bxf", q, k), xf_send.at[k].at[part], xf_recv.at[k].at[part], dict(dx=d))

    def back_z(q):
        a, n = BWD[q]
        recv(("bxf", q, 0))
        recv(("bxf", q, 1))
        for dz in (3, 1, 2, 0):
            total = both(dz * 4, a, n)
            total = total + xf_recv[0, dz, a : a + n].astype(f32) + xf_recv[1, dz, a : a + n].astype(f32)
            if dz:
                z_send[dz - 1, a : a + n] = total.astype(bf16)
                send(("bz", q, dz), z_send.at[dz - 1, pl.ds(a, n)], z_recv.at[dz - 1, pl.ds(a, n)], dict(dzh=STEP[dz]))
            else:
                comb[0, a : a + n] = total

    def back_last(q):
        a, n = BWD[q]
        total = comb[0, a : a + n]
        for dz in (1, 2, 3):
            recv(("bz", q, dz))
            total = total + z_recv[dz - 1, a : a + n].astype(f32)
        fg_t[a : a + n] = total

    weight_1()
    back_products(0)
    weight_2()
    back_xh(0)
    back_products(1)
    weight_3()
    back_xf(0)
    back_xh(1)
    back_products(2)
    weight_4()
    back_xf(1)
    back_z(0)
    back_xh(2)
    back_products(3)
    weight_5()
    back_xf(2)
    back_z(1)
    back_xh(3)
    weight_6()
    back_last(0)
    back_xf(3)
    weight_7()
    back_z(2)
    back_last(1)
    weight_8()
    back_z(3)
    back_last(2)
    back_last(3)
    fgrad_ref[...] = fg_t[...].T.astype(bf16)
    for copy in channels.values():
        copy.wait_send()


def per_device(features, tiles, tile_rows, tile_cols, tile_count, weight, cotangent):
    vmem = pl.BlockSpec(memory_space=pltpu.VMEM)
    smem = pl.BlockSpec(memory_space=pltpu.SMEM)
    square = lambda *lead: pltpu.VMEM((*lead, T, T), bf16)
    wide = lambda *shape: pltpu.VMEM(shape, f32)
    nmax = max(n for _, n in FWD + BWD)
    n_channels = 24 * len(FWD) + 6 * len(FWD) + 18 * len(BWD) + 24
    scratch = [
        square(SLOTS), square(SLOTS), wide(SLOTS, nmax, T), square(8), square(8), wide(T, T), square(), square(), square(),
        square(16), square(16), wide(16, T, T), square(4), square(4), square(2, 4), square(2, 4), square(3), square(3), wide(T, T),
        wide(T, T), wide(128, T), wide(128, T), wide(3, 32, T), wide(32, T), wide(3, 8, T), wide(8, 8, T), wide(32, T),
        wide(128, T), wide(T, T), pltpu.VMEM((8, 128), jnp.int32), pltpu.SMEM((8, 128), jnp.int32),
        pltpu.SemaphoreType.DMA((n_channels,)), pltpu.SemaphoreType.DMA((n_channels,)), pltpu.SemaphoreType.DMA((9,)),
    ]
    scratch += [pltpu.VMEM((32, n, T), bf16) for _, n in FWD]
    scratch += [pltpu.VMEM((8, n, T), bf16) for _, n in BWD]
    return pl.pallas_call(
        kernel,
        name="graph_layer",
        out_shape=(
            jax.ShapeDtypeStruct((T, T), bf16),
            jax.ShapeDtypeStruct((T, T), f32),
            jax.ShapeDtypeStruct((T, T), bf16),
        ),
        in_specs=[vmem, pl.BlockSpec(memory_space=pl.ANY), vmem, vmem, smem, vmem, vmem],
        out_specs=(vmem, vmem, vmem),
        scratch_shapes=scratch,
        compiler_params=pltpu.CompilerParams(
            collective_id=0, has_side_effects=True, vmem_limit_bytes=58 << 20
        ),
    )(
        features,
        tiles.reshape(SLOTS, T, T),
        tile_rows.reshape(1, SLOTS),
        tile_cols.reshape(1, SLOTS),
        tile_count.reshape(1, 1),
        weight,
        cotangent,
    )


def solution(mesh):
    placed = (
        P(("section", "rep"), None),
        P("section", "rep", None, None, None),
        P("section", "rep", None),
        P("section", "rep", None),
        P("section", "rep"),
        P(),
        P(("section", "rep"), None),
    )
    return jax.shard_map(
        per_device,
        mesh=mesh,
        in_specs=placed,
        out_specs=(P(("section", "rep"), None), P(), P(("section", "rep"), None)),
        check_vma=False,
    )
```

time: 667 us -> 108 us (0.16)
  waiting for transfers between devices: 472 us -> 0 us
  Pallas kernels: 0 us -> 101 us
  blocking collectives: 62.8 us -> 0 us
  local copies, waits for them, and re-layouts: 59.2 us -> 4.8 us
  matrix products: 52.8 us -> 0 us
  between operations: 14.5 us -> 1.29 us
    psum x1 -> x0, waiting for transfers between devices: 282 us -> none  [per_device(): weight_grad = lax.psum(weight_terms, 'section')]
    reduce_scatter x1 -> x0, waiting for transfers between devices: 124 us -> none  [per_device(): lax.psum_scatter(column_terms, 'section', scatter_dimension=0, tiled=True)]
    pallas_call x0 -> x1, Pallas kernels: none -> 101 us  [per_device(): pl.pallas_call(kernel, name='graph_layer', out_shape=(jax.ShapeDtypeStruc...]
    all_gather x2 -> x0, waiting for transfers between devices: 64.6 us -> none  [the longest x1 64.6 us: per_device(): gathered = lax.all_gather(features, 'section', axis=0, tiled=True)]
    psum x1 -> x0, blocking collectives: 62.8 us -> none  [per_device(): aggregate = lax.psum(partial_value, 'rep').astype(jnp.bfloat16)]
    dot_general x7 -> x0, matrix products: 52.8 us -> none  [the longest x1 13.9 us: per_device(): jnp.einsum('kji,kjf->kif', section_tiles, chosen, preferred_element_type=...]
    dot_general x4 -> x0, local copies, waits for them, and re-layouts: 44.3 us -> none  [the longest x1 17.8 us: per_device(): jnp.einsum('kij,kjf->kif', section_tiles, selected, preferred_element_typ...]
    gather x2 -> x0, local copies, waits for them, and re-layouts: 13.2 us -> none  [the longest x1 7.72 us: per_device(): selected = gathered.reshape(col_tiles, tile_size, feature_width)[col_ids]]
  transfers between devices with their start and end apart: 4 -> 0, of which waited for: 3 -> 0; matrix products, arithmetic and copies ran while one was open for 8% -> 0% of each run, Pallas kernels for 0% -> 0%
where the time goes in v1:
time: 108 us; the launch traced here: 107 us
  Pallas kernels  101 us (94%)
  local copies, waits for them, and re-layouts  4.8 us (4%)
  between operations  1.29 us (1%)
    pallas_call x1, Pallas kernels, per_device(): pl.pallas_call(kernel, name='graph_layer', out_shape=(jax.ShapeDtypeStruc...  101 us
    unnamed x3, local copies, waits for them, and re-layouts  4.8 us

profile of v1, /device:TPU:1, one launch (start us, length us, event | category | flops | bytes accessed | tf_op | source)
XLA Modules:
  0.0 106.7 jit_solution(16435464133773453972)
XLA Ops:
  1.3 100.6 %graph_layer.1 = (bf16[256,256]{1,0:T(8,128)(2,1)}, f32[256,256]{1,0:T(8,128)}, bf16[256,256]{1,0:T(8,128)(2,1)}) custom-call(bf16[256,256]{1,0:T(8,128)(2,1)} %feat_ref.1, bf16[64,256,256]{2,1,0:T(8,128)(2,1)} %bitcast.3, s32[1,64]{1,0:T(1,128)} %bitcast.4, s32[1,64]{1,0:T(1,128)} %bitcast.5, s32[1,1]{1,0:T(1,128)S(6)} %copy.13.count_ref, ...), custom_call_target="tpu_custom_call" | custom-call | tf_op jit(solution)/shard_map/graph_layer/pallas_call | solution.py:393
  101.9 1.6 %copy.14 = bf16[256,256]{1,0:T(8,128)(2,1)} copy(bf16[256,256]{1,0:T(8,128)(2,1)} %get-tuple-element.6) | data formatting | bytes 262144
  103.4 1.7 %copy.15 = f32[256,256]{1,0:T(8,128)} copy(f32[256,256]{1,0:T(8,128)} %get-tuple-element.7) | data formatting | bytes 524288
  105.1 1.6 %copy.16 = bf16[256,256]{1,0:T(8,128)(2,1)} copy(bf16[256,256]{1,0:T(8,128)(2,1)} %get-tuple-element.8) | data formatting | bytes 262144

commit v2 on v1

--- a/solution.py
+++ b/solution.py
@@ -10,8 +10,10 @@
 SLOTS = 64
 STEP = (0, 1, -1, 2)
 FWD = ((0, 64), (64, 64), (128, 64), (192, 64))
-BWD = ((0, 64), (64, 64), (128, 64), (192, 64))
-UNROLL = 32
+BWD = FWD
+UNROLL = 16
+ARRIVALS = 18 * len(FWD) + 7
+DEPARTURES = 4 * len(FWD) + 7
 
 
 def transpose(v):
@@ -45,19 +47,24 @@
         + rep_offs[1:]
     )
     back = (0, 2, 1, 3)
-    channels = {}
-
-    def send(key, src, dst, off):
-        i = len(channels)
-        copy = pltpu.make_async_remote_copy(
-            src_ref=src, dst_ref=dst, send_sem=send_sem.at[i], recv_sem=recv_sem.at[i],
+    arrivals, departures = {}, {}
+
+    def copy_of(src, dst, out, into, off):
+        return pltpu.make_async_remote_copy(
+            src_ref=src, dst_ref=dst, send_sem=send_sem.at[out], recv_sem=recv_sem.at[into],
             device_id=at(**off), device_id_type=pl.DeviceIdType.MESH,
         )
-        copy.start()
-        channels[key] = copy
-
-    def recv(key):
-        channels[key].wait_recv()
+
+    def send(into, out, src, dst, off):
+        i = arrivals.setdefault(into, len(arrivals))
+        o = departures.setdefault(out, len(departures))
+        copy_of(src, dst, o, i, off).start()
+
+    def recv(into, ref):
+        copy_of(ref, ref, 0, arrivals[into], dict(dx=1)).wait_recv()
+
+    def sent(out, ref):
+        copy_of(ref, ref, departures[out], 0, dict(dx=1)).wait_send()
 
     barrier = pltpu.get_barrier_semaphore()
     for off in partners:
@@ -75,14 +82,20 @@
 
     def x_full(q, dz):
         g = gathered[q]
-        send(("xf", q, dz, 1), g.at[dz * 4], g.at[dz * 4 + 2], dict(dx=1))
-        send(("xf", q, dz, -1), g.at[dz * 4], g.at[dz * 4 + 1], dict(dx=-1))
-
-    for q in range(len(FWD)):
+        send(("xf", q, dz), ("fwd", q), g.at[dz * 4], g.at[dz * 4 + 2], dict(dx=1))
+        send(("xf", q, dz), ("fwd", q), g.at[dz * 4], g.at[dz * 4 + 1], dict(dx=-1))
+
+    def z_full(q):
         g = gathered[q]
-        for dz in (1, 2, 3):
-            send(("z", q, dz), g.at[0], g.at[back[dz] * 4], dict(dzh=STEP[dz]))
-        x_full(q, 0)
+        send(("zf", q, 1), ("fwd", q), g.at[0], g.at[8], dict(dzh=1))
+        send(("zf", q, -1), ("fwd", q), g.at[0], g.at[4], dict(dzh=-1))
+
+    z_full(0)
+    x_full(0, 0)
+    z_full(1)
+    x_full(1, 0)
+    x_full(2, 0)
+    x_full(3, 0)
 
     def make_tables():
         lane = lax.broadcasted_iota(jnp.int32, (SLOTS, SLOTS), 1)
@@ -142,10 +155,6 @@
 
         lax.fori_loop(0, number // 4, step, 0)
 
-    turn(0, 32)
-    wt[...] = transpose(weight_ref[...])
-    cot_t[...] = transpose(cot_ref[...])
-
     def products(source, matrices, base, n):
         def step(i, total):
             for u in range(UNROLL):
@@ -163,133 +172,170 @@
         last = table[base + 3, index]
         return prefix[jnp.clip(last, 0, SLOTS - 1), :n] * jnp.where(last >= 0, 1.0, 0.0)
 
-    def stage_x(q):
-        g, n = gathered[q], FWD[q][1]
-        h = n // 2
-        for dz in (1, 2, 3):
-            recv(("z", q, dz))
-            x_full(q, back[dz])
-        for dz in range(4):
-            recv(("xf", q, dz, 1))
-            send(("xh", q, dz, 1), g.at[dz * 4 + 2, pl.ds(0, h)], g.at[dz * 4 + 3, pl.ds(0, h)], dict(dx=1))
-            recv(("xf", q, dz, -1))
-            send(("xh", q, dz, -1), g.at[dz * 4 + 1, pl.ds(h, h)], g.at[dz * 4 + 3, pl.ds(h, h)], dict(dx=-1))
+    def stage_z(q):
+        g, h = gathered[q], FWD[q][1] // 2
+        recv(("zf", q, 1), g.at[8])
+        send(("zh", q), ("fwd", q), g.at[8, pl.ds(0, h)], g.at[12, pl.ds(0, h)], dict(dzh=1))
+        x_full(q, 2)
+        recv(("zf", q, -1), g.at[4])
+        send(("zh", q), ("fwd", q), g.at[4, pl.ds(h, h)], g.at[12, pl.ds(h, h)], dict(dzh=-1))
+        x_full(q, 1)
+
+    def stage_z_last(q):
+        recv(("zh", q), gathered[q].at[12])
+        x_full(q, 3)
+
+    def stage_xh(q, dz):
+        g, h = gathered[q], FWD[q][1] // 2
+        recv(("xf", q, dz), g.at[pl.ds(dz * 4 + 1, 2)])
+        send(("xh", q, dz), ("fwd", q), g.at[dz * 4 + 2, pl.ds(0, h)], g.at[dz * 4 + 3, pl.ds(0, h)], dict(dx=1))
+        send(("xh", q, dz), ("fwd", q), g.at[dz * 4 + 1, pl.ds(h, h)], g.at[dz * 4 + 3, pl.ds(h, h)], dict(dx=-1))
 
     def stage_core(q):
         g = gathered[q]
-        for dz in range(4):
-            recv(("xh", q, dz, 1))
-            recv(("xh", q, dz, -1))
-            send(("core", q, dz), g.at[pl.ds(dz * 4, 4)], g.at[pl.ds(16 + dz * 4, 4)], dict(dc=1))
+        for dz in (0, 2, 1, 3):
+            recv(("xh", q, dz), g.at[dz * 4 + 3])
+            send(("core", q), ("fwd", q), g.at[pl.ds(dz * 4, 4)], g.at[pl.ds(16 + dz * 4, 4)], dict(dc=1))
 
     def stage_products(q):
         a, n = FWD[q]
-        for dz in range(4):
-            recv(("core", q, dz))
+        recv(("core", q), gathered[q].at[pl.ds(16, 16)])
         products(gathered[q], tiles_t, 0, n)
         for e in (7, 3, 6, 5, 2, 1, 4):
             owner = at(**rep_offs[e])[1]
             rs_send[e, a : a + n] = group(0, owner, n).astype(bf16)
             to = (e // 4) * 4 + back[e % 4]
-            send(("rs", q, e), rs_send.at[e, pl.ds(a, n)], rs_recv.at[to, pl.ds(a, n)], rep_offs[e])
+            send(("rs", q), ("rs", q), rs_send.at[e, pl.ds(a, n)], rs_recv.at[to, pl.ds(a, n)], rep_offs[e])
         agg_own[a : a + n] = group(0, rep, n)
 
-    for q in range(len(FWD) + 1):
-        if q < len(FWD):
-            stage_x(q)
-        if q == 0:
-            turn(32, 32)
-            to_smem.wait()
-        if q >= 1:
-            stage_core(q - 1)
-            stage_products(q - 1)
+    turn(0, 16)
+    z_full(2)
+    stage_xh(0, 0)
+    turn(16, 16)
+    z_full(3)
+    stage_z(0)
+    stage_xh(1, 0)
+    turn(32, 16)
+    stage_z_last(0)
+    stage_z(1)
+    stage_xh(2, 0)
+    stage_xh(0, 2)
+    stage_xh(0, 1)
+    turn(48, 16)
+    stage_z(2)
+    stage_xh(3, 0)
+    stage_xh(1, 2)
+    stage_xh(1, 1)
+    stage_z_last(1)
+    stage_xh(0, 3)
+    stage_z(3)
+    stage_xh(2, 2)
+    stage_xh(2, 1)
+    stage_z_last(2)
+    stage_xh(1, 3)
+    stage_core(0)
+    stage_xh(3, 2)
+    stage_xh(3, 1)
+    stage_z_last(3)
+    to_smem.wait()
+    wt[...] = transpose(weight_ref[...])
+    cot_t[...] = transpose(cot_ref[...])
+    stage_xh(2, 3)
+    stage_core(1)
+    stage_products(0)
+    stage_xh(3, 3)
+    stage_core(2)
+    stage_products(1)
+    stage_core(3)
+    stage_products(2)
+    stage_products(3)
 
     for q, (a, n) in enumerate(FWD):
-        for e in range(1, 8):
-            recv(("rs", q, e))
+        recv(("rs", q), rs_recv.at[pl.ds(1, 7), pl.ds(a, n)])
         total = agg_own[a : a + n]
         for e in range(1, 8):
             total = total + rs_recv[e, a : a + n].astype(f32)
         agg_t[a : a + n] = total.astype(bf16)
+
+    def spread(q):
+        for e in (7, 3, 6, 5, 2, 1, 4):
+            to = (e // 4) * 4 + back[e % 4]
+            send(("ag", q), ("ag", q), row_grads[q].at[0], row_grads[q].at[to], rep_offs[e])
 
     pre = jnp.dot(wt[...], agg_t[...], preferred_element_type=f32)
     sigma = jax.nn.sigmoid(pre)
     pre_grad = (cot_t[...].astype(f32) * (sigma * (1.0 + pre * (1.0 - sigma)))).astype(bf16)
     for q, (a, n) in enumerate(BWD):
         row_grads[q][0] = jnp.dot(weight_ref[a : a + n], pre_grad, preferred_element_type=f32).astype(bf16)
-        for e in (7, 3, 6, 5, 2, 1, 4):
-            to = (e // 4) * 4 + back[e % 4]
-            send(("ag", q, e), row_grads[q].at[0], row_grads[q].at[to], rep_offs[e])
+        if q == 0:
+            spread(0)
     act_ref[...] = (pre * sigma).T.astype(bf16)
     w0[...] = lax.dot_general(agg_t[...], pre_grad, (((1,), (1,)), ((), ())), preferred_element_type=f32)
+    spread(1)
 
     def aligned(v, k):
         return pl.ds(pl.multiple_of(v * k, k), k)
 
     def weight_1():
-        send("w1", w0.at[aligned(1 - c, 128)], w1r, dict(dc=1))
+        send("w1", "w1", w0.at[aligned(1 - c, 128)], w1r, dict(dc=1))
 
     def weight_2():
-        recv("w1")
+        recv("w1", w1r)
         w1[...] = w0[aligned(c, 128), :] + w1r[...]
         for i in (3, 1, 2):
-            send(("w2", i), w1.at[aligned((x + STEP[i] + 4) % 4, 32)], w2r.at[back[i] - 1], dict(dx=STEP[i]))
+            send("w2", "w2", w1.at[aligned((x + STEP[i] + 4) % 4, 32)], w2r.at[back[i] - 1], dict(dx=STEP[i]))
 
     def weight_3():
         total = w1[aligned(x, 32), :]
-        for i in (1, 2, 3):
-            recv(("w2", i))
+        recv("w2", w2r)
         for i in (1, 2, 3):
             total = total + w2r[i - 1]
         w2[...] = total
         for i in (3, 1, 2):
-            send(("w3", i), w2.at[aligned((zh + STEP[i] + 4) % 4, 8)], w3r.at[back[i] - 1], dict(dzh=STEP[i]))
+            send("w3", "w3", w2.at[aligned((zh + STEP[i] + 4) % 4, 8)], w3r.at[back[i] - 1], dict(dzh=STEP[i]))
 
     def weight_4():
         total = w2[aligned(zh, 8), :]
-        for i in (1, 2, 3):
-            recv(("w3", i))
+        recv("w3", w3r)
         for i in (1, 2, 3):
             total = total + w3r[i - 1]
         w4[rep] = total
         for e in range(1, 8):
-            send(("w4", e), w4.at[rep], w4.at[rep], rep_offs[e])
+            send("w4", "w4", w4.at[rep], w4.at[rep], rep_offs[e])
 
     def weight_5():
-        for e in range(1, 8):
-            recv(("w4", e))
+        recv("w4", w4.at[pl.ds(0, 7)])
         w5[aligned(zh, 8), :] = jnp.sum(w4[...], axis=0)
         for i in (3, 1, 2):
-            send(("w5", i), w5.at[aligned(zh, 8)], w5.at[aligned(zh, 8)], dict(dzh=STEP[i]))
+            send("w5", "w5", w5.at[aligned(zh, 8)], w5.at[aligned(zh, 8)], dict(dzh=STEP[i]))
 
     def weight_6():
-        for i in (1, 2, 3):
-            recv(("w5", i))
+        recv("w5", w5.at[pl.ds(0, 24)])
         w6[aligned(x, 32), :] = w5[...]
         for i in (3, 1, 2):
-            send(("w6", i), w6.at[aligned(x, 32)], w6.at[aligned(x, 32)], dict(dx=STEP[i]))
+            send("w6", "w6", w6.at[aligned(x, 32)], w6.at[aligned(x, 32)], dict(dx=STEP[i]))
 
     def weight_7():
-        for i in (1, 2, 3):
-            recv(("w6", i))
+        recv("w6", w6.at[pl.ds(0, 96)])
         w7[aligned(c, 128), :] = w6[...]
-        send("w7", w7.at[aligned(c, 128)], w7.at[aligned(c, 128)], dict(dc=1))
+        send("w7", "w7", w7.at[aligned(c, 128)], w7.at[aligned(c, 128)], dict(dc=1))
 
     def weight_8():
-        recv("w7")
+        recv("w7", w7.at[pl.ds(0, 128)])
         wgrad_ref[...] = w7[...]
 
     def back_products(q):
         a, n = BWD[q]
-        for e in range(1, 8):
-            recv(("ag", q, e))
+        recv(("ag", q), row_grads[q].at[pl.ds(1, 7)])
+        if q + 2 < len(BWD):
+            spread(q + 2)
         products(row_grads[q], tiles, 4, n)
         for dz in (3, 1, 2, 0):
             for dx in (3, 1, 2, 0):
                 other = at(dzh=STEP[dz], dx=STEP[dx], dc=1)[0]
                 c_send[dz * 4 + dx, a : a + n] = group(4, other, n).astype(bf16)
             part = (pl.ds(dz * 4, 4), pl.ds(a, n))
-            send(("bc", q, dz), c_send.at[part], c_recv.at[part], dict(dc=1))
+            send(("bc", q), ("bwd", q), c_send.at[part], c_recv.at[part], dict(dc=1))
         for dz in (3, 1, 2, 0):
             for dx in (3, 1, 2, 0):
                 own = at(dzh=STEP[dz], dx=STEP[dx])[0]
@@ -301,43 +347,42 @@
     def back_xh(q):
         a, n = BWD[q]
         h = n // 2
+        recv(("bc", q), c_recv.at[:, pl.ds(a, n)])
         for dz in range(4):
-            recv(("bc", q, dz))
             xh_send[dz, a : a + n] = both(dz * 4 + 3, a, n).astype(bf16)
         for k, d, s in ((0, 1, a), (1, -1, a + h)):
-            send(("bxh", q, k), xh_send.at[:, pl.ds(s, h)], xh_recv.at[:, pl.ds(s, h)], dict(dx=d))
+            send(("bxh", q), ("bwd", q), xh_send.at[:, pl.ds(s, h)], xh_recv.at[:, pl.ds(s, h)], dict(dx=d))
 
     def back_xf(q):
         a, n = BWD[q]
         h = n // 2
+        recv(("bxh", q), xh_recv.at[:, pl.ds(a, n)])
         for k, d, s in ((0, 1, a), (1, -1, a + h)):
-            recv(("bxh", q, k))
             o = a + h if k == 0 else a
             for dz in range(4):
                 i = dz * 4 + 1 + k
                 xf_send[k, dz, s : s + h] = (both(i, s, h) + xh_recv[dz, s : s + h].astype(f32)).astype(bf16)
                 xf_send[k, dz, o : o + h] = both(i, o, h).astype(bf16)
             part = (slice(None), pl.ds(a, n))
-            send(("bxf", q, k), xf_send.at[k].at[part], xf_recv.at[k].at[part], dict(dx=d))
+            send(("bxf", q), ("bwd", q), xf_send.at[k].at[part], xf_recv.at[k].at[part], dict(dx=d))
 
     def back_z(q):
         a, n = BWD[q]
-        recv(("bxf", q, 0))
-        recv(("bxf", q, 1))
+        recv(("bxf", q), xf_recv.at[:, :, pl.ds(a, n)])
         for dz in (3, 1, 2, 0):
             total = both(dz * 4, a, n)
             total = total + xf_recv[0, dz, a : a + n].astype(f32) + xf_recv[1, dz, a : a + n].astype(f32)
             if dz:
                 z_send[dz - 1, a : a + n] = total.astype(bf16)
-                send(("bz", q, dz), z_send.at[dz - 1, pl.ds(a, n)], z_recv.at[dz - 1, pl.ds(a, n)], dict(dzh=STEP[dz]))
+                send(("bz", q), ("bwd", q), z_send.at[dz - 1, pl.ds(a, n)], z_recv.at[dz - 1, pl.ds(a, n)], dict(dzh=STEP[dz]))
             else:
                 comb[0, a : a + n] = total
 
     def back_last(q):
         a, n = BWD[q]
         total = comb[0, a : a + n]
+        recv(("bz", q), z_recv.at[:, pl.ds(a, n)])
         for dz in (1, 2, 3):
-            recv(("bz", q, dz))
             total = total + z_recv[dz - 1, a : a + n].astype(f32)
         fg_t[a : a + n] = total
 
@@ -347,21 +392,21 @@
     back_xh(0)
     back_products(1)
     weight_3()
+    back_xh(1)
     back_xf(0)
-    back_xh(1)
     back_products(2)
     weight_4()
+    back_xh(2)
     back_xf(1)
-    back_z(0)
-    back_xh(2)
     back_products(3)
     weight_5()
+    back_xh(3)
+    back_z(0)
     back_xf(2)
+    weight_6()
     back_z(1)
-    back_xh(3)
-    weight_6()
+    back_xf(3)
     back_last(0)
-    back_xf(3)
     weight_7()
     back_z(2)
     back_last(1)
@@ -370,8 +415,23 @@
     back_last(2)
     back_last(3)
     fgrad_ref[...] = fg_t[...].T.astype(bf16)
-    for copy in channels.values():
-        copy.wait_send()
+    for q, (a, n) in enumerate(FWD):
+        sent(("fwd", q), gathered[q].at[pl.ds(0, 31)])
+        sent(("rs", q), rs_send.at[pl.ds(1, 7), pl.ds(a, n)])
+        sent(("ag", q), row_grads[q].at[pl.ds(1, 7)])
+        sent(("bwd", q), gathered[q].at[pl.ds(0, 31)])
+    for name, ref in (
+        ("w1", w1r), ("w2", w2r), ("w3", w3r), ("w4", w4.at[pl.ds(0, 7)]),
+        ("w5", w5.at[pl.ds(0, 24)]), ("w6", w6.at[pl.ds(0, 96)]), ("w7", w7.at[pl.ds(0, 128)]),
+    ):
+        sent(name, ref)
+    assert len(arrivals) == ARRIVALS and len(departures) == DEPARTURES
+
+
+def hand_over(a_in, b_in, c_in, a_out, b_out, c_out):
+    a_out[...] = a_in[...]
+    b_out[...] = b_in[...]
+    c_out[...] = c_in[...]
 
 
 def per_device(features, tiles, tile_rows, tile_cols, tile_count, weight, cotangent):
@@ -380,17 +440,16 @@
     square = lambda *lead: pltpu.VMEM((*lead, T, T), bf16)
     wide = lambda *shape: pltpu.VMEM(shape, f32)
     nmax = max(n for _, n in FWD + BWD)
-    n_channels = 24 * len(FWD) + 6 * len(FWD) + 18 * len(BWD) + 24
     scratch = [
         square(SLOTS), square(SLOTS), wide(SLOTS, nmax, T), square(8), square(8), wide(T, T), square(), square(), square(),
         square(16), square(16), wide(16, T, T), square(4), square(4), square(2, 4), square(2, 4), square(3), square(3), wide(T, T),
         wide(T, T), wide(128, T), wide(128, T), wide(3, 32, T), wide(32, T), wide(3, 8, T), wide(8, 8, T), wide(32, T),
         wide(128, T), wide(T, T), pltpu.VMEM((8, 128), jnp.int32), pltpu.SMEM((8, 128), jnp.int32),
-        pltpu.SemaphoreType.DMA((n_channels,)), pltpu.SemaphoreType.DMA((n_channels,)), pltpu.SemaphoreType.DMA((9,)),
+        pltpu.SemaphoreType.DMA((DEPARTURES,)), pltpu.SemaphoreType.DMA((ARRIVALS,)), pltpu.SemaphoreType.DMA((9,)),
     ]
     scratch += [pltpu.VMEM((32, n, T), bf16) for _, n in FWD]
     scratch += [pltpu.VMEM((8, n, T), bf16) for _, n in BWD]
-    return pl.pallas_call(
+    results = pl.pallas_call(
         kernel,
         name="graph_layer",
         out_shape=(
@@ -413,6 +472,13 @@
         weight,
         cotangent,
     )
+    return pl.pallas_call(
+        hand_over,
+        name="hand_over",
+        out_shape=tuple(jax.ShapeDtypeStruct(v.shape, v.dtype) for v in results),
+        in_specs=[vmem] * 3,
+        out_specs=(vmem,) * 3,
+    )(*results)
 
 
 def solution(mesh):

time: 108 us -> 91.3 us (0.85); the launches traced: 107 us -> 91.1 us
  Pallas kernels: 101 us -> 89.8 us
  local copies, waits for them, and re-layouts: 4.8 us -> 0 us
    pallas_call x1, Pallas kernels: 101 us -> 88 us  [per_device(): pl.pallas_call(kernel, name='graph_layer', out_shape=(jax.ShapeDtypeStruc...]
    unnamed x3 -> x0, local copies, waits for them, and re-layouts: 4.8 us -> none
    pallas_call x0 -> x1, Pallas kernels: none -> 1.85 us  [per_device(): pl.pallas_call(hand_over, name='hand_over', out_shape=tuple((jax.ShapeDty...]
where the time goes in v2:
time: 91.3 us; the launch traced here: 91.1 us
  Pallas kernels  89.8 us (98%)
  between operations  1.29 us (1%)
    pallas_call x1, Pallas kernels, per_device(): pl.pallas_call(kernel, name='graph_layer', out_shape=(jax.ShapeDtypeStruc...  88 us
    pallas_call x1, Pallas kernels, per_device(): pl.pallas_call(hand_over, name='hand_over', out_shape=tuple((jax.ShapeDty...  1.85 us

profile of v2, /device:TPU:1, one launch (start us, length us, event | category | flops | bytes accessed | tf_op | source)
XLA Modules:
  0.0 91.1 jit_solution(3151147536230126191)
XLA Ops:
  1.3 88.0 %graph_layer.1 = (bf16[256,256]{1,0:T(8,128)(2,1)}, f32[256,256]{1,0:T(8,128)}, bf16[256,256]{1,0:T(8,128)(2,1)}) custom-call(bf16[256,256]{1,0:T(8,128)(2,1)} %feat_ref.1, bf16[64,256,256]{2,1,0:T(8,128)(2,1)} %bitcast.3, s32[1,64]{1,0:T(1,128)} %bitcast.4, s32[1,64]{1,0:T(1,128)} %bitcast.5, s32[1,1]{1,0:T(1,128)S(6)} %copy.10.count_ref, ...), custom_call_target="tpu_custom_call" | custom-call | tf_op jit(solution)/shard_map/graph_layer/pallas_call | solution.py:452
  89.3 1.8 %hand_over.1 = (bf16[256,256]{1,0:T(8,128)(2,1)}, f32[256,256]{1,0:T(8,128)}, bf16[256,256]{1,0:T(8,128)(2,1)}) custom-call(bf16[256,256]{1,0:T(8,128)(2,1)} %get-tuple-element.6.a_in, f32[256,256]{1,0:T(8,128)} %get-tuple-element.7.b_in, bf16[256,256]{1,0:T(8,128)(2,1)} %get-tuple-element.8.c_in), custom_call_target="tpu_custom_call" | custom-call | tf_op jit(solution)/shard_map/hand_over/pallas_call | solution.py:475

commit v3 on v2

--- a/solution.py
+++ b/solution.py
@@ -208,20 +208,18 @@
             send(("rs", q), ("rs", q), rs_send.at[e, pl.ds(a, n)], rs_recv.at[to, pl.ds(a, n)], rep_offs[e])
         agg_own[a : a + n] = group(0, rep, n)
 
-    turn(0, 16)
     z_full(2)
+    turn(0, 32)
     stage_xh(0, 0)
-    turn(16, 16)
+    stage_z(0)
     z_full(3)
-    stage_z(0)
     stage_xh(1, 0)
-    turn(32, 16)
-    stage_z_last(0)
+    turn(32, 32)
     stage_z(1)
     stage_xh(2, 0)
     stage_xh(0, 2)
     stage_xh(0, 1)
-    turn(48, 16)
+    stage_z_last(0)
     stage_z(2)
     stage_xh(3, 0)
     stage_xh(1, 2)

time: 91.3 us -> 89.2 us (0.977)
  Pallas kernels: 89.8 us -> 87.8 us
    pallas_call x1, Pallas kernels: 88 us -> 85.9 us  [per_device(): pl.pallas_call(kernel, name='graph_layer', out_shape=(jax.ShapeDtypeStruc...]
where the time goes in v3:
time: 89.2 us; the launch traced here: 89 us
  Pallas kernels  87.8 us (98%)
  between operations  1.29 us (1%)
    pallas_call x1, Pallas kernels, per_device(): pl.pallas_call(kernel, name='graph_layer', out_shape=(jax.ShapeDtypeStruc...  85.9 us
    pallas_call x1, Pallas kernels, per_device(): pl.pallas_call(hand_over, name='hand_over', out_shape=tuple((jax.ShapeDty...  1.85 us

profile of v3, /device:TPU:1, one launch (start us, length us, event | category | flops | bytes accessed | tf_op | source)
XLA Modules:
  0.0 89.0 jit_solution(12811281311766010576)
XLA Ops:
  1.3 85.9 %graph_layer.1 = (bf16[256,256]{1,0:T(8,128)(2,1)}, f32[256,256]{1,0:T(8,128)}, bf16[256,256]{1,0:T(8,128)(2,1)}) custom-call(bf16[256,256]{1,0:T(8,128)(2,1)} %feat_ref.1, bf16[64,256,256]{2,1,0:T(8,128)(2,1)} %bitcast.3, s32[1,64]{1,0:T(1,128)} %bitcast.4, s32[1,64]{1,0:T(1,128)} %bitcast.5, s32[1,1]{1,0:T(1,128)S(6)} %copy.10.count_ref, ...), custom_call_target="tpu_custom_call" | custom-call | tf_op jit(solution)/shard_map/graph_layer/pallas_call | solution.py:450
  87.2 1.8 %hand_over.1 = (bf16[256,256]{1,0:T(8,128)(2,1)}, f32[256,256]{1,0:T(8,128)}, bf16[256,256]{1,0:T(8,128)(2,1)}) custom-call(bf16[256,256]{1,0:T(8,128)(2,1)} %get-tuple-element.6.a_in, f32[256,256]{1,0:T(8,128)} %get-tuple-element.7.b_in, bf16[256,256]{1,0:T(8,128)(2,1)} %get-tuple-element.8.c_in), custom_call_target="tpu_custom_call" | custom-call | tf_op jit(solution)/shard_map/hand_over/pallas_call | solution.py:473
